TPU v7x, 256 devices: a whole 4x4x8 slice. The times are simulated.
256 devices in a mesh: dp: 4 (over y), ctx: 8 (over z), head: 8 (over x, core).
Axes of the slice: x: 4, y: 4, z: 8, core: 2. Of those that a mesh axis runs over, the one named last changes fastest.
Arguments:
- query: bfloat16 [4, 1024, 12288], P('dp', 'ctx', 'head'), may hold values from -180 to 180
- latent: bfloat16 [4, 1024, 576], P('dp', ('ctx', 'head')), may hold values from -6 to 6
- w_uk: bfloat16 [512, 8192], P(None, 'head'), may hold values from -0.25 to 0.25
- w_uv: bfloat16 [512, 8192], P(None, 'head'), may hold values from -0.25 to 0.25
- grad_out: bfloat16 [4, 1024, 8192], P('dp', 'ctx', 'head'), may hold values from -6 to 6
- block_order: int32 [16], replicated, may hold values from 0 to 15, as said below
Outputs:
- grad_query: bfloat16 [4, 1024, 12288], P('dp', 'ctx', 'head')
- grad_latent: float32 [4, 1024, 576], P('dp', ('ctx', 'head'))
- grad_w_uk: float32 [512, 8192], P(None, 'head')
- grad_w_uv: float32 [512, 8192], P(None, 'head')
Inputs may be any that keep to these rules, and one draw needn't show every extreme that they name: `block_order`: a permutation of the blocks in which storage blocks 2 r and 2 r + 1 hold blocks whose numbers add up to 15.
All inputs are finite; a program needn't handle non-finite values.
Results may differ from a plain program's by a relative error of at most 0.015.
Values may be sent and summed in bfloat16 or wider, within the bound.
No kernel may reach another device: no remote copies, remote signals or barrier semaphores. Data moves between devices by JAX's collectives and lax.ppermute only.
A program may use at most 64 MiB of HBM per device.

v0:
```python
import jax
import jax.numpy as jnp
from jax import lax
from jax.sharding import PartitionSpec as P

LAT = 512
ROPE = 64
NOPE = 128
VDIM = 128


def split_parts(wide):
    high_part = lax.optimization_barrier(wide.astype(jnp.bfloat16))
    low_part = (wide - high_part.astype(jnp.float32)).astype(jnp.bfloat16)
    return (high_part, low_part)


def contract_cols(left_wide, right):
    high_part, low_part = split_parts(left_wide)
    dims = (((1,), (1,)), ((), ()))
    first = lax.dot_general(high_part, right, dims, preferred_element_type=jnp.float32)
    return first + lax.dot_general(low_part, right, dims, preferred_element_type=jnp.float32)


def contract_rows(left, right_wide):
    high_part, low_part = split_parts(right_wide)
    dims = (((0,), (0,)), ((), ()))
    first = lax.dot_general(left, high_part, dims, preferred_element_type=jnp.float32)
    return first + lax.dot_general(left, low_part, dims, preferred_element_type=jnp.float32)


def project_rows(dkey_flat, dvalue_flat, drope, w_uk, w_uv):
    latent_part = contract_cols(dkey_flat, w_uk) + contract_cols(dvalue_flat, w_uv)
    return jnp.concatenate([latent_part, drope], axis=1)


def on_device(query, latent, w_uk, w_uv, grad_out, block_order):
    q_rows = query[0]
    d_rows = grad_out[0]
    lat = latent[0]
    rows = q_rows.shape[0]
    half = rows // 2
    heads_here = w_uk.shape[1] // NOPE
    width = NOPE + ROPE
    scale = width ** (-0.5)
    rank = lax.axis_index("ctx")
    lat_all = lax.all_gather(lat, ("ctx", "head"), axis=0, tiled=True)
    latent_c = lat_all[:, :LAT]
    keys_flat = jnp.dot(latent_c, w_uk, preferred_element_type=jnp.float32).astype(jnp.bfloat16)
    values_flat = jnp.dot(latent_c, w_uv, preferred_element_type=jnp.float32).astype(jnp.bfloat16)
    rope_all = lat_all[:, LAT:]
    seq = keys_flat.shape[0]
    keys_all = keys_flat.reshape(seq, heads_here, NOPE)
    values_all = values_flat.reshape(seq, heads_here, VDIM)
    q_heads = q_rows.reshape(rows, heads_here, width)
    d_heads = d_rows.reshape(rows, heads_here, VDIM)
    q_nope = q_heads[:, :, :NOPE]
    q_rope = q_heads[:, :, NOPE:]
    key_index = jnp.arange(seq, dtype=jnp.int32)
    key_pos = block_order[key_index // half] * half + key_index % half
    row_index = jnp.arange(rows, dtype=jnp.int32)
    own_block = block_order[2 * rank + row_index // half]
    row_pos = own_block * half + row_index % half
    allowed = (key_pos[None, :] <= row_pos[:, None])[None]
    scores = jnp.einsum("qhn,khn->hqk", q_nope, keys_all, preferred_element_type=jnp.float32)
    scores = scores + jnp.einsum(
        "qhr,kr->hqk", q_rope, rope_all, preferred_element_type=jnp.float32
    )
    scores = scores * scale
    masked = jnp.where(allowed, scores, -jnp.inf)
    top = jnp.max(masked, axis=2, keepdims=True)
    weights = jnp.where(allowed, jnp.exp(masked - top), 0.0)
    probs = weights / jnp.sum(weights, axis=2, keepdims=True)
    probs_b = probs.astype(jnp.bfloat16)
    outputs = jnp.einsum("hqk,khv->qhv", probs_b, values_all, preferred_element_type=jnp.float32)
    drows = jnp.sum(d_heads.astype(jnp.float32) * outputs, axis=2).T
    dprob = jnp.einsum("qhv,khv->hqk", d_heads, values_all, preferred_element_type=jnp.float32)
    dscore = (probs * (dprob - drows[:, :, None])).astype(jnp.bfloat16)
    dq_nope = (
        jnp.einsum("hqk,khn->qhn", dscore, keys_all, preferred_element_type=jnp.float32) * scale
    )
    dq_rope = (
        jnp.einsum("hqk,kr->qhr", dscore, rope_all, preferred_element_type=jnp.float32) * scale
    )
    dkey_all = (
        jnp.einsum("hqk,qhn->khn", dscore, q_nope, preferred_element_type=jnp.float32) * scale
    )
    drope_all = (
        jnp.einsum("hqk,qhr->kr", dscore, q_rope, preferred_element_type=jnp.float32) * scale
    )
    dvalue_all = jnp.einsum("hqk,qhv->khv", probs_b, d_heads, preferred_element_type=jnp.float32)
    grad_q = jnp.concatenate([dq_nope, dq_rope], axis=2)
    grad_query = grad_q.reshape(1, rows, heads_here * width).astype(jnp.bfloat16)
    dkey_flat = dkey_all.reshape(seq, heads_here * NOPE)
    dvalue_flat = dvalue_all.reshape(seq, heads_here * VDIM)
    grad_latent = lax.psum_scatter(
        project_rows(dkey_flat, dvalue_flat, drope_all, w_uk, w_uv),
        ("ctx", "head"),
        scatter_dimension=0,
        tiled=True,
    )
    grad_uk = contract_rows(latent_c, dkey_flat)
    grad_uv = contract_rows(latent_c, dvalue_flat)
    grad_w_uk, grad_w_uv = lax.psum((grad_uk, grad_uv), ("dp", "ctx"))
    return (grad_query, grad_latent[None], grad_w_uk, grad_w_uv)


def solution(mesh):
    return jax.shard_map(
        on_device,
        mesh=mesh,
        in_specs=(
            P("dp", "ctx", "head"),
            P("dp", ("ctx", "head"), None),
            P(None, "head"),
            P(None, "head"),
            P("dp", "ctx", "head"),
            P(),
        ),
        out_specs=(
            P("dp", "ctx", "head"),
            P("dp", ("ctx", "head"), None),
            P(None, "head"),
            P(None, "head"),
        ),
        check_vma=False,
    )
```

profile of v0, /device:TPU:2, one launch (start us, length us, event | category | flops | bytes accessed | tf_op | source)
XLA Modules:
  0.0 496.9 jit_solution(8960798203634442078)
XLA Ops:
  7.2 0.0 copy-start
  7.2 0.0 all-gather.3.cloned.1.call-start
  7.2 0.7 all-gather.3.cloned.1.call-update
  7.9 0.0 all-reduce.5.cloned.1.call-start
  8.0 1.1 copy.50
  9.1 0.0 copy-start.13
  9.1 1.3 copy.47
  10.7 1.9 fusion.35
  12.7 10.1 %fusion.31 = s32[128]{0:T(128)S(1)} fusion(s32[]{:T(128)} %bitcast.11, s32[]{:T(128)} %bitcast.12, s32[]{:T(128)} %bitcast.13, s32[]{:T(128)} %bitcast.14, s32[]{:T(128)} %bitcast.15, s32[]{:T(128)} %bitcast.17, s32[]{:T(128)} %bitcast.16, s32[]{:T(128)} %bitcast.2, s32[]{:T(128)} %bitcast.3, s32[]{:T(128)} %bitcast.4, s32[]{:T(128)} %bitcast.5, s32[]{:T(128)} %bitcast.6, ...), kind=kLoop, calls=%fused_computation.98 | loop fusion | flops 6400 | bytes 580 | tf_op jit(solution)/shard_map/add | solution.py:63
  22.7 4.3 compare_select_fusion.1
  27.1 5.7 %fusion.27 = s32[1024]{0:T(1024)S(1)} fusion(pred[1024]{0:T(1024)(128)(4,1)S(1)} %compare_reduce_fusion, pred[1024]{0:T(1024)(128)(4,1)S(1)} %compare_reduce_fusion.1, pred[1024]{0:T(1024)(128)(4,1)S(1)} %compare_reduce_fusion.2, pred[1024]{0:T(1024)(128)(4,1)S(1)} %compare_reduce_fusion.3, pred[1024]{0:T(1024)(128)(4,1)S(1)} %compare_reduce_fusion.4, ...), kind=kLoop, calls=%fused_computation.71 | loop fusion | flops 17408 | bytes 17444 | tf_op jit(solution)/shard_map/add | solution.py:60
  32.8 0.2 broadcast_compare_fusion
  33.0 56.4 %all-gather.3.cloned.1.call-done = bf16[1,1024,576]{2,1,0:T(8,128)(2,1)} async-done(((bf16[1,16,576]{2,1,0:T(8,128)(2,1)}), bf16[1,1024,576]{2,1,0:T(8,128)(2,1)}) %all-gather.3.cloned.1.call-update) | async-done | bytes 1179664 | tf_op jit(solution)/shard_map/all_gather | solution.py:47
  89.4 1.6 copy.46
  91.0 4.3 convolution_convert_fusion
  95.3 1.3 convolution_convert_fusion.1
  96.6 0.0 copy-start.1
  96.6 1.3 copy-done.1
  97.9 2.7 fusion.22
  100.7 5.8 %fusion.36 = (f32[8,128]{1,0:T(8,128)S(1)}, f32[8,128,1024]{1,2,0:T(8,128)}) fusion(pred[128,1024]{0,1:T(8,128)(4,1)S(1)} %broadcast_compare_fusion, f32[8,1024,128]{2,1,0:T(8,128)} %fusion.22, bf16[128,8,192]{0,2,1:T(8,128)(2,1)S(1)} %bitcast.190, bf16[1024,576]{0,1:T(8,128)(2,1)S(1)} %bitcast.196), kind=kOutput, calls=%fused_computation.103 | convolution fusion | flops 140510208 | bytes 8916992 | tf_op jit(solution)/shard_map/sub | solution.py:72
  106.5 2.7 fusion.6
  109.2 0.1 copy-done.16
  109.4 0.7 fusion.9
  110.1 1.5 copy-done.6
  111.5 2.1 fusion.3
  113.6 0.8 fusion.11
  114.4 0.0 copy-start.14
  114.4 0.7 convolution_multiply_fusion
  115.1 0.2 copy-done.14
  115.3 0.7 fusion.39
  116.0 0.3 bitcast_convert_fusion
  116.3 0.8 fusion.1
  117.2 0.4 copy-done.11
  117.6 2.7 fusion.15
  120.3 1.3 fusion.42
  121.5 0.5 bitcast_convert_fusion.1
  122.0 0.0 copy-start.3
  122.0 0.8 fusion.2
  122.9 0.5 copy-done.3
  123.4 1.3 fusion.40
  124.7 0.1 copy-done.8
  124.8 1.3 fusion.41
  126.1 1.4 add_add_fusion
  127.5 1.5 pad_maximum_fusion
  129.0 0.0 all-reduce.5.cloned.1.call-update
  129.1 0.0 all-reduce.7.cloned.1.call-start
  129.1 3.3 fusion.18
  132.5 0.2 copy-done.18
  132.6 2.7 add_bitcast_fusion
  135.3 2.6 add_bitcast_fusion.1
  137.9 0.0 all-reduce.7.cloned.1.call-update
  137.9 0.7 copy-done.17
  138.6 0.6 dynamic-slice
  139.8 0.0 copy-start.2
  139.8 1.5 fusion.13
  141.4 0.1 copy-done.2
  141.5 0.7 fusion.10
  142.3 0.9 copy.60
  143.2 174.6 %all-reduce.5.cloned.1.call-done = f32[1024,576]{0,1:T(8,128)} async-done(((f32[1024,576]{0,1:T(8,128)}), f32[1024,576]{0,1:T(8,128)}) %all-reduce.5.cloned.1.call-update) | async-done | bytes 2359312
  317.8 1.1 dynamic-slice_bitcast_fusion
  318.9 0.8 copy.61
  319.6 165.9 %all-reduce.7.cloned.1.call-done = (f32[512,1024]{0,1:T(8,128)}, f32[512,1024]{0,1:T(8,128)}) async-done(((f32[512,1024]{0,1:T(8,128)}, f32[512,1024]{0,1:T(8,128)}), (f32[512,1024]{0,1:T(8,128)}, f32[512,1024]{0,1:T(8,128)})) %all-reduce.7.cloned.1.call-update) | async-done | bytes 4194320 | tf_op jit(solution)/shard_map/psum | solution.py:104
  485.6 3.0 copy.62
  488.6 1.8 copy.63
  (32 shorter events, 0.4 us)
Async XLA Ops:
  7.2 88.1 %copy-start = (bf16[512,1024]{1,0:T(8,128)(2,1)S(1)}, bf16[512,1024]{1,0:T(8,128)(2,1)}, u32[]{:S(2)}) copy-start(bf16[512,1024]{1,0:T(8,128)(2,1)} %param.8) | copy-start | bytes 3145732
  7.2 82.2 %all-gather.3.cloned.1.call-start = ((), (), s32[]{:S(2)}) async-start(), calls=%async_computation | async-start | bytes 1331200 | tf_op jit(solution)/shard_map/all_gather | solution.py:47
  7.9 309.9 %all-reduce.5.cloned.1.call-start = ((), (), s32[]{:S(2)}) async-start(), calls=%async_computation.1 | async-start | bytes 4718592
  9.1 100.1 %copy-start.13 = (bf16[1,128,1024]{1,2,0:T(8,128)(2,1)}, bf16[1,128,1024]{1,2,0:T(8,128)(2,1)S(1)}, u32[]{:S(2)}) copy-start(bf16[1,128,1024]{1,2,0:T(8,128)(2,1)S(1)} %copy.50) | copy-start | bytes 786436
  91.0 9.7 %copy-start.10 = (bf16[1,1024,576]{1,2,0:T(8,128)(2,1)}, bf16[1,1024,576]{1,2,0:T(8,128)(2,1)S(1)}, u32[]{:S(2)}) copy-start(bf16[1,1024,576]{1,2,0:T(8,128)(2,1)S(1)} %copy.46) | copy-start | bytes 3538948
  96.6 1.3 copy-start.1
  106.5 2.9 copy-start.16
  109.4 2.2 copy-start.6
  114.4 1.0 copy-start.14
  116.3 1.3 copy-start.11
  117.6 8.4 %copy-start.4 = (bf16[1024,1024]{0,1:T(8,128)(2,1)}, bf16[1024,1024]{0,1:T(8,128)(2,1)S(1)}, u32[]{:S(2)}) copy-start(bf16[1024,1024]{0,1:T(8,128)(2,1)S(1)} %fusion.1) | copy-start | bytes 6291460
  117.6 2.7 copy-start.15
  122.0 1.4 copy-start.3
  123.4 1.4 copy-start.8
  129.1 356.5 %all-reduce.7.cloned.1.call-start = ((), (), s32[]{:S(2)}) async-start(), calls=%async_computation.2 | async-start | bytes 8388608 | tf_op jit(solution)/shard_map/psum | solution.py:104
  129.1 3.3 copy-start.5
  129.1 3.3 copy-start.12
  129.1 3.5 copy-start.18
  132.6 2.7 copy-start.9
  137.9 0.7 copy-start.17
  139.8 1.7 copy-start.2
  485.6 3.0 copy-start.7
Sparse Core Ops, SparseCore 0:
  10.7 78.6 all-gather.2
  129.2 188.5 all-reduce.4
  322.1 163.4 all-reduce.6
where the time goes:
time: 498 us; the launch traced here: 497 us
  waiting for transfers between devices  398 us (80%)
  matrix products  37.8 us (8%)
  other arithmetic  27.3 us (5%)
  local copies, waits for them, and re-layouts  19.3 us (4%)
  between operations  14.7 us (3%)
    unnamed x4, waiting for transfers between devices  175 us
    psum x1, waiting for transfers between devices, on_device(): grad_w_uk, grad_w_uv = lax.psum((grad_uk, grad_uv), ('dp', 'ctx'))  166 us
    all_gather x1, waiting for transfers between devices, on_device(): lat_all = lax.all_gather(lat, ('ctx', 'head'), axis=0, tiled=True)  56.4 us
    unnamed x45, local copies, waits for them, and re-layouts  14.7 us
    add x1, other arithmetic, on_device(): row_pos = own_block * half + row_index % half  10.1 us
  transfers between devices with their start and end apart: 3, of which 3 were waited for; matrix products, arithmetic and copies ran while one was open for 8% of the time, Pallas kernels for 0%

commit v1 on v0

--- a/solution.py
+++ b/solution.py
@@ -44,7 +44,15 @@
     width = NOPE + ROPE
     scale = width ** (-0.5)
     rank = lax.axis_index("ctx")
-    lat_all = lax.all_gather(lat, ("ctx", "head"), axis=0, tiled=True)
+    ways, here = (lax.axis_size(("ctx", "head")), lax.axis_index(("ctx", "head")))
+    grown, reach = (lat, 1)
+    while reach < ways:
+        theirs = lax.ppermute(grown, ("ctx", "head"), [(d, d ^ reach) for d in range(ways)])
+        mine_first = jnp.concatenate([grown, theirs], axis=0)
+        theirs_first = jnp.concatenate([theirs, grown], axis=0)
+        grown = jnp.where(here & reach == 0, mine_first, theirs_first)
+        reach = 2 * reach
+    lat_all = grown
     latent_c = lat_all[:, :LAT]
     keys_flat = jnp.dot(latent_c, w_uk, preferred_element_type=jnp.float32).astype(jnp.bfloat16)
     values_flat = jnp.dot(latent_c, w_uv, preferred_element_type=jnp.float32).astype(jnp.bfloat16)

time: 498 us -> 482 us (0.968)
  waiting for transfers between devices: 398 us -> 371 us
  starting transfers between devices: 0.12 us -> 13.9 us
    all_gather x1 -> x0, waiting for transfers between devices: 56.4 us -> none  [on_device(): lat_all = lax.all_gather(lat, ('ctx', 'head'), axis=0, tiled=True)]
    ppermute x0 -> x6, waiting for transfers between devices: none -> 29.8 us  [on_device(): lax.ppermute(grown, ('ctx', 'head'), [(d, d ^ reach) for d in range(ways)])]
    ppermute x0 -> x6, starting transfers between devices: none -> 13.8 us  [on_device(): lax.ppermute(grown, ('ctx', 'head'), [(d, d ^ reach) for d in range(ways)])]
    unnamed x45 -> x53, local copies, waits for them, and re-layouts: 14.7 us -> 13.6 us
    unnamed x4 -> x3, waiting for transfers between devices: 175 us -> 175 us
  transfers between devices with their start and end apart: 3 -> 8, of which waited for: 3 -> 7; matrix products, arithmetic and copies ran while one was open for 8% -> 8% of each run, Pallas kernels for 0% -> 0%
where the time goes in v1:
time: 482 us; the launch traced here: 481 us
  waiting for transfers between devices  371 us (77%)
  matrix products  36.3 us (8%)
  other arithmetic  29.4 us (6%)
  local copies, waits for them, and re-layouts  15.7 us (3%)
  between operations  15.1 us (3%)
  starting transfers between devices  13.9 us (3%)
    unnamed x3, waiting for transfers between devices  175 us
    psum x1, waiting for transfers between devices, on_device(): grad_w_uk, grad_w_uv = lax.psum((grad_uk, grad_uv), ('dp', 'ctx'))  166 us
    ppermute x6, waiting for transfers between devices, on_device(): lax.ppermute(grown, ('ctx', 'head'), [(d, d ^ reach) for d in range(ways)])  29.8 us
    ppermute x6, starting transfers between devices, on_device(): lax.ppermute(grown, ('ctx', 'head'), [(d, d ^ reach) for d in range(ways)])  13.8 us
    unnamed x53, local copies, waits for them, and re-layouts  13.6 us
    add x1, other arithmetic, on_device(): row_pos = own_block * half + row_index % half  10.1 us
  transfers between devices with their start and end apart: 8, of which 7 were waited for; matrix products, arithmetic and copies ran while one was open for 8% of the time, Pallas kernels for 0%

profile of v1, /device:TPU:2, one launch (start us, length us, event | category | flops | bytes accessed | tf_op | source)
XLA Modules:
  0.0 481.2 jit_solution(15321252621576109431)
XLA Ops:
  7.4 1.4 collective-permute-done
  8.7 0.8 pad_maximum_fusion.3
  9.9 2.4 collective-permute-start.1
  12.2 4.2 collective-permute-done.1
  16.4 0.2 maximum_select_fusion.3
  16.6 1.7 collective-permute-start.2
  18.3 5.3 %collective-permute-done.2 = bf16[64,576]{0,1:T(8,128)(2,1)S(1)} collective-permute-done((bf16[64,576]{0,1:T(8,128)(2,1)S(1)}, bf16[64,576]{0,1:T(8,128)(2,1)S(1)}, u32[]{:S(2)}, u32[]{:S(2)}) %collective-permute-start.2) | collective-permute-done | bytes 73760 | tf_op jit(solution)/shard_map/ppermute | solution.py:50
  23.6 0.2 maximum_select_fusion.4
  23.8 1.2 collective-permute-start.3
  25.0 4.0 collective-permute-done.3
  29.1 2.6 collective-permute-start.4
  31.6 0.2 copy.47
  31.8 0.2 copy.44
  32.1 0.7 fusion.35
  32.8 10.1 %fusion.31 = s32[128]{0:T(128)S(1)} fusion(s32[]{:T(128)} %bitcast.11, s32[]{:T(128)} %bitcast.12, s32[]{:T(128)} %bitcast.13, s32[]{:T(128)} %bitcast.14, s32[]{:T(128)} %bitcast.15, s32[]{:T(128)} %bitcast.17, s32[]{:T(128)} %bitcast.16, s32[]{:T(128)} %bitcast.2, s32[]{:T(128)} %bitcast.3, s32[]{:T(128)} %bitcast.4, s32[]{:T(128)} %bitcast.5, ...), kind=kLoop, calls=%fused_computation.106 | loop fusion | flops 6400 | bytes 580 | tf_op jit(solution)/shard_map/add | solution.py:71
  43.1 5.9 %collective-permute-start.5 = (bf16[512,576]{0,1:T(8,128)(2,1)S(1)}, bf16[512,576]{0,1:T(8,128)(2,1)S(1)}, u32[]{:S(2)}, u32[]{:S(2)}) collective-permute-start(bf16[512,576]{0,1:T(8,128)(2,1)S(1)} %maximum_select_fusion.1), channel_id=1, source_target_pairs={{0,32},{1,33},{2,34},{3,35},{4,36},{5,37},{6,38},{7,39},{8,40},{9,... | collective-permute-start | bytes 1769480 | tf_op jit(solution)/shard_map/ppermute | solution.py:50
  49.2 0.2 compare_reduce_fusion
  49.4 4.3 compare_select_fusion.1
  53.8 5.7 %fusion.27 = s32[1024]{0:T(1024)S(1)} fusion(pred[1024]{0:T(1024)(128)(4,1)S(1)} %compare_reduce_fusion, pred[1024]{0:T(1024)(128)(4,1)S(1)} %compare_reduce_fusion.1, pred[1024]{0:T(1024)(128)(4,1)S(1)} %compare_reduce_fusion.2, pred[1024]{0:T(1024)(128)(4,1)S(1)} %compare_reduce_fusion.3, pred[1024]{0:T(1024)(128)(4,1)S(1)} %compare_reduce_fusion.4, ...), kind=kLoop, calls=%fused_computation.79 | loop fusion | flops 17408 | bytes 17444 | tf_op jit(solution)/shard_map/add | solution.py:68
  59.5 0.2 broadcast_compare_fusion
  59.7 14.9 %collective-permute-done.5 = bf16[512,576]{0,1:T(8,128)(2,1)S(1)} collective-permute-done((bf16[512,576]{0,1:T(8,128)(2,1)S(1)}, bf16[512,576]{0,1:T(8,128)(2,1)S(1)}, u32[]{:S(2)}, u32[]{:S(2)}) %collective-permute-start.5) | collective-permute-done | bytes 589856 | tf_op jit(solution)/shard_map/ppermute | solution.py:50
  74.6 0.3 maximum_select_fusion
  75.0 2.6 convolution_convert_fusion
  77.6 1.3 convolution_convert_fusion.1
  78.9 1.3 copy-done.1
  80.3 2.7 fusion.22
  83.0 5.8 %fusion.36 = (f32[8,128]{1,0:T(8,128)S(1)}, f32[8,128,1024]{1,2,0:T(8,128)}) fusion(pred[128,1024]{0,1:T(8,128)(4,1)S(1)} %broadcast_compare_fusion, f32[8,1024,128]{2,1,0:T(8,128)} %fusion.22, bf16[128,8,192]{0,2,1:T(8,128)(2,1)S(1)} %bitcast.186, bf16[1024,576]{0,1:T(8,128)(2,1)S(1)} %maximum_select_fusion), kind=kOutput, calls=%fused_computation.111 | convolution fusion | flops 140510208 | bytes 8916992 | tf_op jit(solution)/shard_map/sub | solution.py:80
  88.8 2.7 fusion.6
  91.5 0.1 copy-done.20
  91.7 0.7 fusion.9
  92.4 1.5 copy-done.7
  93.9 2.1 fusion.3
  96.0 0.8 fusion.11
  96.7 0.7 convolution_multiply_fusion
  97.4 0.2 copy-done.14
  97.7 0.7 fusion.39
  98.4 0.3 bitcast_convert_fusion
  98.7 0.8 fusion.1
  99.5 0.5 copy-done.3
  100.1 0.6 copy-done.16
  100.7 1.3 fusion.42
  101.9 0.3 bitcast_convert_fusion.1
  102.2 1.1 fusion.2
  103.3 0.3 copy-done.5
  103.6 1.3 fusion.40
  104.9 0.7 copy-done.11
  105.6 2.7 fusion.14
  108.3 1.3 fusion.41
  109.6 1.5 add_add_fusion
  111.1 1.7 pad_maximum_fusion
  112.8 3.3 fusion.17
  116.3 2.7 convolution_add_fusion
  119.0 2.6 convolution_add_fusion.1
  121.7 0.6 copy-done.21
  122.3 0.6 dynamic-slice
  123.6 1.5 fusion.13
  125.2 0.7 fusion.10
  126.0 0.9 copy.57
  126.9 175.1 %all-reduce.5.cloned.1.call-done = f32[1024,576]{0,1:T(8,128)} async-done(((f32[1024,576]{0,1:T(8,128)}), f32[1024,576]{0,1:T(8,128)}) %all-reduce.5.cloned.1.call-update) | async-done | bytes 2359312
  302.0 1.1 dynamic-slice_bitcast_fusion
  303.1 0.8 copy.58
  303.8 165.9 %all-reduce.7.cloned.1.call-done = (f32[512,1024]{1,0:T(8,128)}, f32[512,1024]{1,0:T(8,128)}) async-done(((f32[512,1024]{1,0:T(8,128)}, f32[512,1024]{1,0:T(8,128)}), (f32[512,1024]{1,0:T(8,128)}, f32[512,1024]{1,0:T(8,128)})) %all-reduce.7.cloned.1.call-update) | async-done | bytes 4194320 | tf_op jit(solution)/shard_map/psum | solution.py:112
  469.8 3.3 copy.75
  473.1 1.3 copy.76
  (57 shorter events, 1.4 us)
Async XLA Ops:
  7.2 70.5 %copy-start = (bf16[512,1024]{1,0:T(8,128)(2,1)S(1)}, bf16[512,1024]{1,0:T(8,128)(2,1)}, u32[]{:S(2)}) copy-start(bf16[512,1024]{1,0:T(8,128)(2,1)} %param.8) | copy-start | bytes 3145732
  7.2 24.5 %copy-start.18 = (bf16[1,128,1024]{2,1,0:T(8,128)(2,1)S(1)}, bf16[1,128,1024]{2,1,0:T(8,128)(2,1)}, u32[]{:S(2)}) copy-start(bf16[1,128,1024]{2,1,0:T(8,128)(2,1)} %param.10) | copy-start | bytes 786436
  7.2 24.6 %copy-start.17 = (bf16[1,128,1536]{2,1,0:T(8,128)(2,1)S(1)}, bf16[1,128,1536]{2,1,0:T(8,128)(2,1)}, u32[]{:S(2)}) copy-start(bf16[1,128,1536]{2,1,0:T(8,128)(2,1)} %param.6) | copy-start | bytes 1179652
  7.2 24.9 %copy-start.19 = (s32[16]{0:T(128)S(1)}, s32[16]{0:T(128)}, u32[]{:S(2)}) copy-start(s32[16]{0:T(128)} %param.11) | copy-start | bytes 196
  7.2 294.8 %all-reduce.5.cloned.1.call-start = ((), (), s32[]{:S(2)}) async-start(), calls=%async_computation | async-start | bytes 4718592
  7.3 1.5 collective-permute-start
  9.9 6.5 %collective-permute-start.1 = (bf16[32,576]{0,1:T(8,128)(2,1)S(1)}, bf16[32,576]{0,1:T(8,128)(2,1)S(1)}, u32[]{:S(2)}, u32[]{:S(2)}) collective-permute-start(bf16[32,576]{0,1:T(8,128)(2,1)S(1)} %broadcast_select_fusion), channel_id=1, source_target_pairs={{0,2},{1,3},{2,0},{3,1},{4,6},{5,7},{6,4},{7,5},{8,10},{9,11},{10,... | collective-permute-start | bytes 110600 | tf_op jit(solution)/shard_map/ppermute | solution.py:50
  16.6 7.0 %collective-permute-start.2 = (bf16[64,576]{0,1:T(8,128)(2,1)S(1)}, bf16[64,576]{0,1:T(8,128)(2,1)S(1)}, u32[]{:S(2)}, u32[]{:S(2)}) collective-permute-start(bf16[64,576]{0,1:T(8,128)(2,1)S(1)} %maximum_select_fusion.3), channel_id=1, source_target_pairs={{0,4},{1,5},{2,6},{3,7},{4,0},{5,1},{6,2},{7,3},{8,12},{9,13},{10,... | collective-permute-start | bytes 221192 | tf_op jit(solution)/shard_map/ppermute | solution.py:50
  23.8 5.2 %collective-permute-start.3 = (bf16[128,576]{0,1:T(8,128)(2,1)S(1)}, bf16[128,576]{0,1:T(8,128)(2,1)S(1)}, u32[]{:S(2)}, u32[]{:S(2)}) collective-permute-start(bf16[128,576]{0,1:T(8,128)(2,1)S(1)} %maximum_select_fusion.4), channel_id=1, source_target_pairs={{0,8},{1,9},{2,10},{3,11},{4,12},{5,13},{6,14},{7,15},{8,0},{9,1},... | collective-permute-start | bytes 442376 | tf_op jit(solution)/shard_map/ppermute | solution.py:50
  29.1 13.8 %collective-permute-start.4 = (bf16[256,576]{0,1:T(8,128)(2,1)S(1)}, bf16[256,576]{0,1:T(8,128)(2,1)S(1)}, u32[]{:S(2)}, u32[]{:S(2)}) collective-permute-start(bf16[256,576]{0,1:T(8,128)(2,1)S(1)} %maximum_select_fusion.2), channel_id=1, source_target_pairs={{0,16},{1,17},{2,18},{3,19},{4,20},{5,21},{6,22},{7,23},{8,24},{9,... | collective-permute-start | bytes 884744 | tf_op jit(solution)/shard_map/ppermute | solution.py:50
  31.8 59.7 %copy-start.13 = (bf16[1,128,1024]{1,2,0:T(8,128)(2,1)}, bf16[1,128,1024]{1,2,0:T(8,128)(2,1)S(1)}, u32[]{:S(2)}) copy-start(bf16[1,128,1024]{1,2,0:T(8,128)(2,1)S(1)} %copy.47) | copy-start | bytes 786436
  32.1 42.9 %copy-start.15 = (bf16[512,1024]{1,0:T(8,128)(2,1)S(1)}, bf16[512,1024]{1,0:T(8,128)(2,1)}, u32[]{:S(2)}) copy-start(bf16[512,1024]{1,0:T(8,128)(2,1)} %param.9) | copy-start | bytes 3145732
  43.1 31.6 %collective-permute-start.5 = (bf16[512,576]{0,1:T(8,128)(2,1)S(1)}, bf16[512,576]{0,1:T(8,128)(2,1)S(1)}, u32[]{:S(2)}, u32[]{:S(2)}) collective-permute-start(bf16[512,576]{0,1:T(8,128)(2,1)S(1)} %maximum_select_fusion.1), channel_id=1, source_target_pairs={{0,32},{1,33},{2,34},{3,35},{4,36},{5,37},{6,38},{7,39},{8,40},{9,... | collective-permute-start | bytes 1769480 | tf_op jit(solution)/shard_map/ppermute | solution.py:50
  75.0 8.0 %copy-start.10 = (bf16[1024,576]{0,1:T(8,128)(2,1)}, bf16[1024,576]{0,1:T(8,128)(2,1)S(1)}, u32[]{:S(2)}) copy-start(bf16[1024,576]{0,1:T(8,128)(2,1)S(1)} %maximum_select_fusion) | copy-start | bytes 3538948
  78.9 1.3 copy-start.1
  88.8 2.9 copy-start.20
  91.7 2.2 copy-start.7
  96.7 1.0 copy-start.14
  98.7 1.4 copy-start.3
  98.7 2.0 copy-start.16
  102.2 1.4 copy-start.5
  103.6 4.7 copy-start.9
  103.6 2.0 copy-start.11
  112.8 357.0 %all-reduce.7.cloned.1.call-start = ((), (), s32[]{:S(2)}) async-start(), calls=%async_computation.1 | async-start | bytes 8388608 | tf_op jit(solution)/shard_map/psum | solution.py:112
  112.8 3.4 copy-start.4
  112.8 3.4 copy-start.12
  112.8 3.5 copy-start.22
  116.3 2.7 copy-start.6
  121.6 0.7 copy-start.21
  123.6 1.7 copy-start.2
  469.8 3.3 copy-start.8
Sparse Core Ops, SparseCore 0:
  112.9 189.0 all-reduce.4
  306.3 163.4 all-reduce.6
